TPU v7x, 32 devices: a whole 2x2x4 slice. The times are simulated.
32 devices in a mesh: groups: 2 (over x), ctx: 8 (over z, y), chan: 2 (over core).
Axes of the slice: x: 2, y: 2, z: 4, core: 2. Of those that a mesh axis runs over, the one named last changes fastest.
Arguments:
- tokens: int32 [4, 512], P('groups', 'ctx'), parts along dimension 0, may hold values from 0 to 511
- embed_table: bfloat16 [512, 4096], replicated, may hold values from -8 to 8
- norm_gain: float32 [4096], replicated, may hold values from 0.1 to 1.9
- input_proj: bfloat16 [4096, 3, 2048], P('ctx', None, 'chan'), may hold values from -0.09375 to 0.09375
- short_filter: float32 [3, 128, 3], P(None, 'chan'), may hold values from -3.5 to 3.5
- pole_rate: float32 [128, 16], P('chan'), may hold values from 0.0005859375 to 0.2
- residue: float32 [128, 16], P('chan'), may hold values from -1.5 to 1.5
- skip_gain: float32 [2048], P('chan'), may hold values from -3 to 3
- output_proj: bfloat16 [2048, 4096], P('chan', 'ctx'), may hold values from -0.125 to 0.125
Outputs:
- block_out: bfloat16 [4, 512, 4096], P('groups', 'ctx', 'chan'), parts along dimension 0
There are 2 independent parts, one for each index of `groups`. A program takes and returns all parts, laid end to end along the dimension named above; an argument that names none is the same for every part. Nothing has to cross between parts.
All inputs are finite; a program needn't handle non-finite values.
Results may differ from a plain program's by a relative error of at most 0.0078.
Values may be sent and summed in bfloat16 or wider, within the bound.
A program may use at most 128 MiB of HBM per device.

v0:
```python
import jax
import jax.numpy as jnp
from jax import lax
from jax.sharding import PartitionSpec as P

epsilon = 1e-06
highest = lax.Precision.HIGHEST


def passed_along(shard, axis, by):
    count = lax.axis_size(axis)
    pairs = [(i, i + by) for i in range(count) if 0 <= i + by < count]
    return lax.ppermute(shard, axis, pairs)


def entering(shard, axis, combine, identity):
    count, mine = (lax.axis_size(axis), lax.axis_index(axis))
    everything = jax.tree.map(lambda part: lax.all_gather(part, axis), shard)
    start = jax.tree.map(
        lambda part, zero: jnp.broadcast_to(jnp.asarray(zero, part.dtype), part.shape),
        shard,
        identity,
    )

    def hop(k, before):
        reached = k < mine
        new = combine(before, jax.tree.map(lambda part: part[k], everything))
        return jax.tree.map(lambda a, b: jnp.where(reached, a, b), new, before)

    return lax.fori_loop(0, count, hop, start)


def local_block(operands):
    rising, falling, inputs = operands
    length = rising.shape[2]
    toeplitz = jnp.einsum("gnt,gns->gts", rising, falling, precision=highest)
    causal = jnp.arange(length)[:, None] >= jnp.arange(length)[None, :]
    toeplitz = jnp.where(causal[None], toeplitz, 0.0)
    return jnp.einsum("gms,gts->gmt", inputs, toeplitz, precision=highest)


def lookup_rows(token_block, embed_table):
    vocab_count = embed_table.shape[0]
    onehot = (token_block[:, None] == jnp.arange(vocab_count, dtype=jnp.int32)[None, :]).astype(
        jnp.bfloat16
    )
    return jnp.dot(onehot, embed_table, preferred_element_type=jnp.float32)


def body(
    tokens,
    embed_table,
    norm_gain,
    input_proj,
    short_filter,
    pole_rate,
    residue,
    skip_gain,
    output_proj,
):
    genome_count, row_count = tokens.shape
    part_rows, branch_count, channels = input_proj.shape
    groups = pole_rate.shape[0]
    group_size = channels // groups
    tap_count = short_filter.shape[2]
    flat_count = genome_count * row_count
    flat_tokens = tokens.reshape(flat_count)
    widened = lookup_rows(flat_tokens, embed_table)
    inv_rms = lax.rsqrt(jnp.mean(widened * widened, axis=-1, keepdims=True) + epsilon)
    normed = (widened * inv_rms * norm_gain).astype(jnp.bfloat16)
    proj_cols = branch_count * channels
    flat_weight = input_proj.reshape(part_rows, proj_cols)
    spread = lax.all_to_all(normed, "ctx", split_axis=1, concat_axis=0, tiled=True)
    summed = lax.psum_scatter(
        jnp.dot(spread, flat_weight, preferred_element_type=jnp.float32),
        "ctx",
        scatter_dimension=0,
        tiled=True,
    )
    projected = summed.astype(jnp.bfloat16).reshape(genome_count, row_count, branch_count, channels)
    rim = passed_along(projected[:, row_count - (tap_count - 1) :], "ctx", 1)
    extended = jnp.concatenate([rim, projected], axis=1).astype(jnp.float32)
    taps_full = jnp.broadcast_to(
        short_filter[:, :, None, :], (branch_count, groups, group_size, tap_count)
    ).reshape(branch_count, channels, tap_count)
    filtered = jnp.zeros((genome_count, row_count, branch_count, channels), jnp.float32)
    for lag in range(tap_count):
        first_row = tap_count - 1 - lag
        filtered = filtered + taps_full[:, :, lag] * extended[:, first_row : first_row + row_count]
    query_part = filtered[:, :, 0]
    product = filtered[:, :, 1] * filtered[:, :, 2]
    mixes = genome_count * group_size
    grouped = (
        product.reshape(genome_count, row_count, groups, group_size)
        .transpose(2, 0, 3, 1)
        .reshape(groups, mixes, row_count)
    )
    positions = jnp.arange(row_count, dtype=jnp.float32)
    middle = float(row_count // 2)
    powers = jnp.exp(-pole_rate[:, :, None] * positions)
    next_powers = jnp.exp(-pole_rate[:, :, None] * (positions + 1.0))
    pole_amp = residue * jnp.sqrt(-jnp.expm1(-2.0 * pole_rate))
    rising = pole_amp[:, :, None] * jnp.exp(-pole_rate[:, :, None] * (positions - middle))
    falling = jnp.exp(-pole_rate[:, :, None] * (middle - positions))
    block_size = 8
    blocks = groups // block_size
    poles = pole_rate.shape[1]
    local_part = lax.map(
        local_block,
        (
            rising.reshape(blocks, block_size, poles, row_count),
            falling.reshape(blocks, block_size, poles, row_count),
            grouped.reshape(blocks, block_size, mixes, row_count),
        ),
    )
    local_part = local_part.reshape(groups, mixes, row_count)
    end_state = jnp.einsum("gms,gns->gmn", grouped, powers[:, :, ::-1], precision=highest)
    block_decay = jnp.exp(-pole_rate * row_count)

    def combine(earlier, later):
        return (earlier[0] * later[0], later[0][:, None, :] * earlier[1] + later[1])

    identity = (jnp.ones_like(block_decay), jnp.zeros_like(end_state))
    incoming = entering((block_decay, end_state), "ctx", combine, identity)[1]
    weighted = incoming * pole_amp[:, None, :]
    correction = jnp.einsum("gmn,gnt->gmt", weighted, next_powers, precision=highest)
    long_conv = (
        (local_part + correction)
        .reshape(groups, genome_count, group_size, row_count)
        .transpose(1, 3, 0, 2)
        .reshape(genome_count, row_count, channels)
    )
    gated = (
        (query_part * (long_conv + skip_gain * product))
        .astype(jnp.bfloat16)
        .reshape(flat_count, channels)
    )
    partial_value = jnp.dot(
        gated,
        lax.all_gather(output_proj, "ctx", axis=1, tiled=True),
        preferred_element_type=jnp.float32,
    )
    own_share = lax.psum_scatter(partial_value, "chan", scatter_dimension=1, tiled=True)
    half_width = own_share.shape[1]
    residual_part = lax.dynamic_slice_in_dim(
        widened, lax.axis_index("chan") * half_width, half_width, 1
    )
    block_out = (residual_part + own_share).astype(jnp.bfloat16)
    return block_out.reshape(genome_count, row_count, half_width)


def solution(mesh):
    return jax.shard_map(
        body,
        mesh=mesh,
        in_specs=(
            P("groups", "ctx"),
            P(),
            P(),
            P("ctx", None, "chan"),
            P(None, "chan", None),
            P("chan", None),
            P("chan", None),
            P("chan"),
            P("chan", "ctx"),
        ),
        out_specs=P("groups", "ctx", "chan"),
        check_vma=False,
    )
```

profile of v0, /device:TPU:1, one launch (start us, length us, event | category | flops | bytes accessed | tf_op | source)
XLA Modules:
  0.0 502.0 jit_solution(10771387078758091748)
XLA Ops:
  7.3 3.0 multiply_reduce_fusion
  11.7 6.4 %all-to-all-start = ((bf16[128,8,512]{2,0,1:T(8,128)(2,1)}), bf16[128,8,512]{2,0,1:T(8,128)(2,1)S(1)}, u32[]{:S(2)}, u32[]{:S(2)}) async-start(bf16[128,8,512]{2,0,1:T(8,128)(2,1)} %bitcast.64), calls=%async_computation | async-start | bytes 2097152 | tf_op jit(solution)/shard_map/all_to_all | solution.py:73
  18.1 4.7 copy.61
  22.8 19.9 %all-to-all-done = bf16[128,8,512]{2,0,1:T(8,128)(2,1)S(1)} async-done(((bf16[128,8,512]{2,0,1:T(8,128)(2,1)}), bf16[128,8,512]{2,0,1:T(8,128)(2,1)S(1)}, u32[]{:S(2)}, u32[]{:S(2)}) %all-to-all-start) | async-done | bytes 1048608 | tf_op jit(solution)/shard_map/all_to_all | solution.py:73
  42.7 8.3 %fusion.22 = f32[1024,3072]{1,0:T(8,128)} fusion(bf16[1024,512]{1,0:T(8,128)(2,1)S(1)} %bitcast.92, bf16[512,3072]{0,1:T(8,128)(2,1)} %bitcast.88), kind=kOutput, calls=%fused_computation.54 | convolution fusion | flops 3221225472 | bytes 16777216 | tf_op jit(solution)/shard_map/dot_general | solution.py:75
  53.7 205.3 %reduce-scatter.3.cloned.1.call-done = f32[128,3072]{1,0:T(8,128)} async-done(((f32[1024,3072]{1,0:T(8,128)}), f32[128,3072]{1,0:T(8,128)}) %reduce-scatter.3.cloned.1.call-update) | async-done | bytes 1572880 | tf_op jit(solution)/shard_map/reduce_scatter | solution.py:74
  259.0 2.4 convert_element_type.18
  261.4 2.7 reshape.90
  264.2 3.1 collective-permute-start
  267.3 2.0 rev.3
  270.7 1.8 slice_multiply_fusion.3
  272.5 1.3 copy.62
  273.7 1.4 copy.63
  275.1 3.6 fusion.23
  279.8 24.6 %all-gather.2 = f32[8,64,16]{1,2,0:T(8,128)S(1)} all-gather(f32[1,64,16]{1,2,0:T(8,128)S(1)} %copy.66), channel_id=2, replica_groups=mesh['groups'=2,'ctx'=8,'chan'=2] {'ctx'}, dimensions={0}, use_global_device_ids=true | all-gather | bytes 36864 | tf_op jit(solution)/shard_map/all_gather | solution.py:18
  304.4 2.1 multiply_exponential_fusion.1
  306.5 1.9 copy.77
  308.4 2.0 copy.71
  310.4 1.9 copy.76
  312.4 2.2 copy.72
  314.6 21.5 %while.24 = (s32[]{:T(128)}, f32[8,8,32,64]{3,2,1,0:T(8,128)}, f32[8,8,32,64]{3,2,1,0:T(8,128)S(1)}, f32[8,8,16,64]{3,2,1,0:T(8,128)}, f32[8,8,16,64]{3,2,1,0:T(8,128)}, /*index=5*/s32[]{:T(128)}) while((s32[]{:T(128)}, f32[8,8,32,64]{3,2,1,0:T(8,128)}, f32[8,8,32,64]{3,2,1,0:T(8,128)S(1)}, f32[8,8,16,64]{3,2,1,0:T(8,128)}, ...), condition=%wide.region_3.4_spmd, body=%wide.region_2.3_spmd.sunk | while | flops 18911232 | bytes 796741 | solution.py:108
  314.6 1.5 convolution_select_fusion.2
  316.1 1.2 fusion.42
  317.3 1.5 convolution_select_fusion.2
  318.7 1.2 fusion.42
  319.9 1.5 convolution_select_fusion.2
  321.4 1.2 fusion.42
  322.6 1.5 convolution_select_fusion.2
  324.1 1.2 fusion.42
  325.3 1.5 convolution_select_fusion.2
  326.8 1.2 fusion.42
  328.0 1.5 convolution_select_fusion.2
  329.5 1.2 fusion.42
  330.7 1.5 convolution_select_fusion.2
  332.2 1.2 fusion.42
  333.4 1.5 convolution_select_fusion.2
  334.9 1.2 fusion.42
  336.0 15.4 %all-gather.8.cloned.1.call-done = f32[512,32,16]{1,2,0:T(8,128)} async-done(((f32[64,32,16]{1,2,0:T(8,128)}), f32[512,32,16]{1,2,0:T(8,128)}) %all-gather.8.cloned.1.call-update) | async-done | bytes 1048592 | tf_op jit(solution)/shard_map/all_gather | solution.py:18
  351.4 4.5 copy.68
  355.9 9.6 %while.25 = (s32[]{:T(128)}, f32[64,32,16]{0,2,1:T(8,128)S(1)}, s32[]{:T(128)}, f32[8,64,16]{1,2,0:T(8,128)S(1)}, f32[8,64,32,16]{1,3,2,0:T(8,128)}, /*index=5*/s32[]{:T(128)}, s32[]{:T(128)}) while((s32[]{:T(128)}, f32[64,32,16]{0,2,1:T(8,128)S(1)}, s32[]{:T(128)}, f32[8,64,16]{1,2,0:T(8,128)S(1)}, f32[8,64,32,16]{1,3,2,0:T(8,128)}, ...), condition=%wide.region_5.6_spmd.clone, body=%wide.region_4.5_spmd.clone.sunk | while | flops 131076 | bytes 405609 | solution.py:30
  359.5 1.2 fusion.43
  360.7 1.2 fusion.43
  365.8 3.2 convolution_add_fusion
  369.6 1.4 reshape.94
  371.0 106.9 %all-gather.6.cloned.1.call-done = bf16[1024,4096]{1,0:T(8,128)(2,1)} async-done(((bf16[1024,512]{1,0:T(8,128)(2,1)}), bf16[1024,4096]{1,0:T(8,128)(2,1)}) %all-gather.6.cloned.1.call-update) | async-done | bytes 8388624 | tf_op jit(solution)/shard_map/all_gather | solution.py:140
  477.9 6.7 %fusion.14 = f32[128,4096]{1,0:T(8,128)} fusion(bf16[1024,4096]{1,0:T(8,128)(2,1)} %all-gather.6.cloned.1.call-done, f32[128,1024]{0,1:T(8,128)} %copy.72, f32[128,1024]{0,1:T(8,128)} %reshape.94, f32[128,1024]{0,1:T(8,128)} %copy.71, f32[1024]{0:T(1024)S(1)} %copy-done.1), kind=kOutput, calls=%fused_computation.34 | convolution fusion | flops 1074266112 | bytes 12062720 | tf_op jit(solution)/shard_map/dot_general | solution.py:138
  484.6 8.8 %reduce-scatter.5.cloned.1.call-done = f32[128,2048]{1,0:T(8,128)} async-done(((f32[128,4096]{1,0:T(8,128)}), f32[128,2048]{1,0:T(8,128)}) %reduce-scatter.5.cloned.1.call-update) | async-done | bytes 1048592 | tf_op jit(solution)/shard_map/reduce_scatter | solution.py:143
  493.3 2.1 add_convert_fusion
  (68 shorter events, 15.1 us)
Async XLA Ops:
  7.3 3.1 copy-start.3
  11.7 31.0 %all-to-all-start = ((bf16[128,8,512]{2,0,1:T(8,128)(2,1)}), bf16[128,8,512]{2,0,1:T(8,128)(2,1)S(1)}, u32[]{:S(2)}, u32[]{:S(2)}) async-start(bf16[128,8,512]{2,0,1:T(8,128)(2,1)} %bitcast.64), calls=%async_computation | async-start | bytes 2097152 | tf_op jit(solution)/shard_map/all_to_all | solution.py:73
  18.1 240.9 %reduce-scatter.3.cloned.1.call-start = ((), (), s32[]{:S(2)}) async-start(), calls=%async_computation.3 | async-start | bytes 14155776 | tf_op jit(solution)/shard_map/reduce_scatter | solution.py:74
  51.0 0.7 copy-start.5
  51.0 1.0 copy-start.2
  51.0 300.4 %all-gather.8.cloned.1.call-start = ((), (), s32[]{:S(2)}) async-start(), calls=%async_computation.6 | async-start | bytes 4718592 | tf_op jit(solution)/shard_map/all_gather | solution.py:18
  264.2 5.2 %collective-permute-start = (bf16[2,2,3,1024]{3,2,1,0:T(4,128)(2,1)S(1)}, bf16[2,2,3,1024]{3,2,1,0:T(4,128)(2,1)S(1)}, u32[]{:S(2)}, u32[]{:S(2)}) collective-permute-start(bf16[2,2,3,1024]{3,2,1,0:T(4,128)(2,1)S(1)} %slice.41), channel_id=1, source_target_pairs={{0,2},{2,4},{4,6},{6,8},{8,10},{10,12},{12,14},{1,3},{3,5},{5,7},{... | collective-permute-start | bytes 73736 | tf_op jit(solution)/shard_map/ppermute | solution.py:13
  272.5 1.3 copy-start
  275.1 4.5 copy-start.4
  278.8 199.1 %all-gather.6.cloned.1.call-start = ((), (), s32[]{:S(2)}) async-start(), calls=%async_computation.4 | async-start | bytes 9437184 | tf_op jit(solution)/shard_map/all_gather | solution.py:140
  279.5 213.8 %reduce-scatter.5.cloned.1.call-start = ((), (), s32[]{:S(2)}) async-start(), calls=%async_computation.5 | async-start | bytes 3145728 | tf_op jit(solution)/shard_map/reduce_scatter | solution.py:143
  369.1 108.8 %copy-start.1 = (f32[1024]{0:T(1024)S(1)}, f32[1024]{0:T(1024)}, u32[]{:S(2)}) copy-start(f32[1024]{0:T(1024)} %param.20) | copy-start | bytes 12292
Sparse Core Ops, SparseCore 0:
  51.1 207.8 reduce-scatter.2
  278.9 72.4 all-gather.7
  353.5 124.3 all-gather.5
  484.7 8.5 reduce-scatter.4
where the time goes:
time: 504 us; the launch traced here: 502 us
  waiting for transfers between devices  357 us (71%)
  matrix products  46.2 us (9%)
  local copies, waits for them, and re-layouts  30 us (6%)
  blocking collectives  24.6 us (5%)
  other arithmetic  21 us (4%)
  between operations  13.3 us (3%)
  starting transfers between devices  9.63 us (2%)
    reduce_scatter x1, waiting for transfers between devices, body(): lax.psum_scatter(jnp.dot(spread, flat_weight, preferred_element_type=jnp....  205 us
    all_gather x1, waiting for transfers between devices, body(): lax.all_gather(output_proj, 'ctx', axis=1, tiled=True)  107 us
    all_gather x1, blocking collectives, entering(): everything = jax.tree.map(lambda part: lax.all_gather(part, axis), shard)  24.6 us
    all_to_all x1, waiting for transfers between devices, body(): lax.all_to_all(normed, 'ctx', split_axis=1, concat_axis=0, tiled=True)  19.9 us
    all_gather x1, waiting for transfers between devices, entering(): everything = jax.tree.map(lambda part: lax.all_gather(part, axis), shard)  15.4 us
    unnamed x20, local copies, waits for them, and re-layouts  13.9 us
    dot_general x8, matrix products, local_block(): toeplitz = jnp.einsum('gnt,gns->gts', rising, falling, precision=highest)  11.9 us
  transfers between devices with their start and end apart: 6, of which 5 were waited for; matrix products, arithmetic and copies ran while one was open for 12% of the time, Pallas kernels for 0%

commit v1 on v0

v1 whole, which is shorter than its diff:
```python
import functools

import jax
import jax.numpy as jnp
from jax import lax
from jax.experimental import pallas as pl
from jax.experimental.pallas import tpu as pltpu
from jax.sharding import PartitionSpec as P

EPSILON = 1e-06
LANES = 128
MESH = pl.DeviceIdType.MESH
F32 = jnp.float32
BF16 = jnp.bfloat16


def remote(src, dst, send_sem, recv_sem, where):
    return pltpu.make_async_remote_copy(
        src_ref=src,
        dst_ref=dst,
        send_sem=send_sem,
        recv_sem=recv_sem,
        device_id=where,
        device_id_type=MESH,
    )


def kernel(
    sizes,
    tok_ref,
    norm_ref,
    w_ref,
    taps_ref,
    rate_ref,
    amp_ref,
    skip_ref,
    wout_ref,
    table_ref,
    out_ref,
    tok_all,
    tok_col,
    part_y,
    part_own,
    recv_y,
    recv_r,
    recv_l,
    sum_z,
    vocab_proj,
    toeplitz,
    conv,
    gathered,
    acc,
    recv_c,
    obuf,
    land,
    table_cols,
    tok_send,
    tok_recv,
    ysend,
    yrecv,
    zsend,
    rrecv,
    lrecv,
    gsend,
    grecv,
    ar_send,
    al_send,
    ay_send,
    arecv,
    csend,
    crecv,
    osend,
    orecv,
    local_sem,
):
    groups, ctx, chans, ny, group_size = sizes
    nz = ctx // ny
    genomes, local_len = tok_ref.shape
    length = local_len * ctx
    rows = norm_ref.shape[0]
    vocab = rows * groups
    cols = wout_ref.shape[1]
    poles = rate_ref.shape[1]
    filters = rate_ref.shape[0]
    half = length // chans
    per = ctx // chans

    gi = lax.axis_index("groups")
    me = lax.axis_index("ctx")
    ci = lax.axis_index("chan")
    y = lax.rem(me, ny)
    z = me // ny
    other_y = z * ny + (ny - 1 - y)
    right, left = me + ny, me - ny
    dest_chan = me // per

    barrier = pltpu.get_barrier_semaphore()

    def greet(where):
        pl.semaphore_signal(barrier, inc=1, device_id=where, device_id_type=MESH)

    for off in range(1, ctx):
        greet({"ctx": lax.rem(me + off, ctx)})
    for off in range(1, groups):
        greet({"groups": lax.rem(gi + off, groups)})
    greet({"chan": 1 - ci})
    for q in range(per):
        target = ci * per + q

        @pl.when(jnp.logical_or(target != me, dest_chan != ci))
        def _():
            greet({"ctx": target, "chan": dest_chan})

    table_copy = pltpu.make_async_copy(
        table_ref.at[:, pl.ds(pl.multiple_of(me * cols, LANES), cols)], table_cols, local_sem.at[0]
    )
    table_copy.start()
    self_target = jnp.where(dest_chan == ci, 1, 0)
    pl.semaphore_wait(barrier, ctx - 1 + groups - 1 + 1 + per - self_target)

    tok_all[me] = tok_ref[...]
    for off in range(1, ctx):
        peer = lax.rem(me + off, ctx)
        remote(
            tok_ref, tok_all.at[me], tok_send.at[off], tok_recv.at[me], {"ctx": peer}
        ).start()

    def project(block, branch):
        columns = pl.ds(pl.multiple_of(block * LANES, LANES), LANES)
        return jnp.dot(norm_ref[...], w_ref[branch, :, columns], preferred_element_type=F32)

    order = []
    for step in range((nz + 1) // 2):
        order.append(nz - 1 - step)
        if step != nz - 1 - step:
            order.append(step)
    if ny == 2:
        for dz in order:
            for branch in range(3):
                part_y[dz, :, branch * LANES : (branch + 1) * LANES] = project(
                    dz * ny + 1 - y, branch
                ).astype(BF16)
            remote(
                part_y.at[dz], recv_y.at[dz], ysend.at[dz], yrecv.at[dz], {"ctx": other_y}
            ).start()
    for dz in order:
        for branch in range(3):
            part_own[dz, :, branch * LANES : (branch + 1) * LANES] = project(dz * ny + y, branch)

    def with_y(dz):
        value = part_own[dz]
        if ny == 2:
            remote(
                part_y.at[dz], recv_y.at[dz], ysend.at[dz], yrecv.at[dz], {"ctx": other_y}
            ).wait_recv()
            value = value + recv_y[dz].astype(F32)
        return value

    def right_copy(dz):
        return remote(sum_z.at[dz], recv_r.at[dz], zsend.at[dz], rrecv.at[dz], {"ctx": right})

    def left_copy(dz):
        return remote(sum_z.at[dz], recv_l.at[dz], zsend.at[dz], lrecv.at[dz], {"ctx": left})

    for step in range(nz - 1):
        dr, dl = nz - 1 - step, step

        @pl.when(z < dr)
        def _():
            part_own[dr] = with_y(dr)

            @pl.when(z > 0)
            def _():
                right_copy(dr).wait_recv()
                part_own[dr] = part_own[dr] + recv_r[dr].astype(F32)

            sum_z[dr] = part_own[dr].astype(BF16)
            right_copy(dr).start()

        @pl.when(z > dl)
        def _():
            part_own[dl] = with_y(dl)

            @pl.when(z < nz - 1)
            def _():
                left_copy(dl).wait_recv()
                part_own[dl] = part_own[dl] + recv_l[dl].astype(F32)

            sum_z[dl] = part_own[dl].astype(BF16)
            left_copy(dl).start()

    width = length + LANES
    lag = length - 1 - lax.broadcasted_iota(jnp.int32, (poles, width), 1)
    lag_f = jnp.maximum(lag, 0).astype(F32)
    for f in range(filters):
        taps = jnp.sum(amp_ref[f] * jnp.exp(-rate_ref[f] * lag_f), axis=0, keepdims=True)
        taps = jnp.where(lag[:1] >= 0, taps, 0.0)
        rolled = pltpu.roll(
            jnp.broadcast_to(taps, (LANES, width)), width - (LANES - 1), 1, stride=1, stride_axis=0
        )
        toeplitz[f] = rolled[:, :length].astype(BF16)

    for off in range(1, ctx):
        peer = lax.rem(me + off, ctx)
        remote(
            tok_ref, tok_all.at[peer], tok_send.at[off], tok_recv.at[peer], {"ctx": peer}
        ).wait_recv()
    for b in range(genomes):
        line = jnp.concatenate([tok_all[i, b : b + 1, :] for i in range(ctx)], axis=1)
        tok_col[b] = jnp.transpose(jnp.broadcast_to(line, (LANES, length)))

    own = with_y(z)
    part_own[z] = own

    @pl.when(z > 0)
    def _():
        right_copy(z).wait_recv()
        part_own[z] = part_own[z] + recv_r[z].astype(F32)

    @pl.when(z < nz - 1)
    def _():
        left_copy(z).wait_recv()
        part_own[z] = part_own[z] + recv_l[z].astype(F32)

    vocab_proj[gi] = part_own[z].astype(BF16)

    def group_copy(off):
        return remote(
            vocab_proj.at[gi],
            vocab_proj.at[gi],
            gsend.at[off],
            grecv.at[gi],
            {"groups": lax.rem(gi + off, groups)},
        )

    for off in range(1, groups):
        group_copy(off).start()
    for off in range(1, groups):
        peer = lax.rem(gi + off, groups)
        remote(
            vocab_proj.at[peer],
            vocab_proj.at[peer],
            gsend.at[off],
            grecv.at[peer],
            {"groups": peer},
        ).wait_recv()

    table_proj = vocab_proj[...].reshape(vocab, 3 * LANES)

    def onehot(columns):
        parts = []
        for v in range(vocab // LANES):
            ids = lax.broadcasted_iota(jnp.int32, columns.shape, 1) + v * LANES
            parts.append(jnp.where(columns == ids, 1.0, 0.0).astype(BF16))
        return jnp.concatenate(parts, axis=1)

    row_ids = lax.broadcasted_iota(jnp.int32, (length, LANES), 0)
    queries, products = [], []
    for b in range(genomes):
        projected = jnp.dot(onehot(tok_col[b]), table_proj, preferred_element_type=F32)
        filtered = []
        for branch in range(3):
            value = projected[:, branch * LANES : (branch + 1) * LANES]
            total = taps_ref[branch * 3 : branch * 3 + 1, :] * value
            for k in (1, 2):
                shifted = jnp.where(row_ids >= k, pltpu.roll(value, k, 0), 0.0)
                at = branch * 3 + k
                total = total + taps_ref[at : at + 1, :] * shifted
            filtered.append(total)
        queries.append(filtered[0])
        products.append(filtered[1] * filtered[2])
    both = jnp.concatenate(products, axis=1)
    lane_filter = lax.rem(
        lax.broadcasted_iota(jnp.int32, (length, genomes * LANES), 1), LANES
    ) // group_size
    blocks = length // LANES
    for f in range(filters):
        masked = jnp.where(lane_filter == f, both, 0.0).astype(BF16)
        for i in range(blocks):
            term = jnp.dot(
                toeplitz[f, :, (blocks - 1 - i) * LANES :],
                masked[: (i + 1) * LANES],
                preferred_element_type=F32,
            )
            at = slice(i * LANES, (i + 1) * LANES)
            conv[at, :] = term if f == 0 else conv[at, :] + term
    for b in range(genomes):
        long_conv = conv[:, b * LANES : (b + 1) * LANES]
        gated = queries[b] * (long_conv + skip_ref[...] * products[b])
        gathered[me, b] = gated.astype(BF16)

    def along(slot, sems, where):
        return remote(
            gathered.at[slot], gathered.at[slot], sems.at[slot], arecv.at[slot], {"ctx": where}
        )

    @pl.when(z < nz - 1)
    def _():
        along(me, ar_send, right).start()

    @pl.when(z > 0)
    def _():
        along(me, al_send, left).start()

    if ny == 2:
        along(me, ay_send, other_y).start()

    acc[...] = jnp.zeros_like(acc)

    def multiply(slot):
        weight = wout_ref[pl.ds(pl.multiple_of(slot * LANES, LANES), LANES), :]
        for b in range(genomes):
            acc[b] = acc[b] + jnp.dot(gathered[slot, b], weight, preferred_element_type=F32)

    multiply(me)

    @pl.loop(1, nz)
    def _(step):
        from_left = me - step * ny
        from_right = me + step * ny

        @pl.when(from_left >= 0)
        def _():
            along(from_left, ar_send, right).wait_recv()

            @pl.when(z < nz - 1)
            def _():
                along(from_left, ar_send, right).start()

            if ny == 2:
                along(from_left, ay_send, other_y).start()

        @pl.when(from_right < ctx)
        def _():
            along(from_right, al_send, left).wait_recv()

            @pl.when(z > 0)
            def _():
                along(from_right, al_send, left).start()

            if ny == 2:
                along(from_right, ay_send, other_y).start()

        @pl.when(from_left >= 0)
        def _():
            multiply(from_left)

        @pl.when(from_right < ctx)
        def _():
            multiply(from_right)

    if ny == 2:

        @pl.loop(0, nz)
        def _(step):
            twin_z = lax.rem(z + step, nz)
            slot = twin_z * ny + (1 - y)
            along(slot, ay_send, other_y).wait_recv()
            multiply(slot)

    swap = remote(
        acc.at[:, pl.ds(pl.multiple_of((1 - ci) * half, LANES), half), :],
        recv_c,
        csend.at[0],
        crecv.at[0],
        {"chan": 1 - ci},
    )
    swap.start()
    table_copy.wait()
    mine = pl.ds(pl.multiple_of(ci * half, LANES), half)
    for b in range(genomes):
        land_tok = tok_col[b, mine, :]
        acc[b, mine, :] = acc[b, mine, :] + jnp.dot(
            onehot(land_tok), table_cols[...], preferred_element_type=F32
        )
    swap.wait()
    for b in range(genomes):
        obuf[b] = (acc[b, mine, :] + recv_c[b]).astype(BF16)

    def out_copy(q, source_slot):
        return remote(
            obuf.at[:, pl.ds(q * local_len, local_len), :],
            land.at[source_slot],
            osend.at[q],
            orecv.at[source_slot],
            {"ctx": ci * per + q, "chan": dest_chan},
        )

    def is_self(q):
        return jnp.logical_and(ci * per + q == me, dest_chan == ci)

    my_slot = lax.rem(me, per)
    for q in range(per):

        @pl.when(jnp.logical_not(is_self(q)))
        def _():
            out_copy(q, my_slot).start()

        @pl.when(is_self(q))
        def _():
            land[my_slot] = obuf[:, q * local_len : (q + 1) * local_len, :]

    for q in range(per):

        @pl.when(jnp.logical_not(is_self(q)))
        def _():
            out_copy(q, q).wait_recv()

        out_ref[:, :, q * cols : (q + 1) * cols] = land[q]

    for q in range(per):

        @pl.when(jnp.logical_not(is_self(q)))
        def _():
            out_copy(q, my_slot).wait_send()

    for off in range(1, ctx):
        remote(
            tok_ref, tok_all.at[me], tok_send.at[off], tok_recv.at[me], {"ctx": lax.rem(me + off, ctx)}
        ).wait_send()
    for off in range(1, groups):
        group_copy(off).wait_send()
    for dz in range(nz):
        if ny == 2:
            remote(
                part_y.at[dz], recv_y.at[dz], ysend.at[dz], yrecv.at[dz], {"ctx": other_y}
            ).wait_send()

        @pl.when(z < dz)
        def _():
            right_copy(dz).wait_send()

        @pl.when(z > dz)
        def _():
            left_copy(dz).wait_send()

        slot = dz * ny + y

        @pl.when(jnp.logical_and(dz <= z, z < nz - 1))
        def _():
            along(slot, ar_send, right).wait_send()

        @pl.when(jnp.logical_and(dz >= z, z > 0))
        def _():
            along(slot, al_send, left).wait_send()

        if ny == 2:
            along(slot, ay_send, other_y).wait_send()


def body(
    groups,
    ctx,
    chans,
    tokens,
    embed_table,
    norm_gain,
    input_proj,
    short_filter,
    pole_rate,
    residue,
    skip_gain,
    output_proj,
):
    genomes, local_len = tokens.shape
    length = local_len * ctx
    features, branches, channels = input_proj.shape
    vocab = embed_table.shape[0]
    filter_count, poles = pole_rate.shape
    group_size = channels // filter_count
    share = channels // ctx
    filters = filter_count // ctx
    cols = output_proj.shape[1]
    rows = vocab // groups
    ny = 2 if ctx % 2 == 0 and ctx <= 8 else 1
    nz = ctx // ny
    taps = short_filter.shape[2]
    me = lax.axis_index("ctx")
    gi = lax.axis_index("groups")
    half = length // chans
    per = ctx // chans

    own_rows = lax.dynamic_slice_in_dim(embed_table, gi * rows, rows, 0)
    wide = own_rows.astype(F32)
    inv_rms = lax.rsqrt(jnp.mean(wide * wide, axis=-1, keepdims=True) + EPSILON)
    own_feats = lax.dynamic_slice_in_dim(own_rows, me * features, features, 1).astype(F32)
    gain = lax.dynamic_slice_in_dim(norm_gain, me * features, features, 0)
    normed = (own_feats * inv_rms * gain).astype(BF16)

    def padded(array):
        if share == LANES:
            return array
        cut = array.reshape(array.shape[:-1] + (ctx, share))
        pads = [(0, 0)] * (cut.ndim - 1) + [(0, LANES - share)]
        return jnp.pad(cut, pads).reshape(array.shape[:-1] + (ctx * LANES,))

    def own_share(array):
        wide_array = jnp.repeat(array, group_size, axis=-1)
        return jnp.pad(wide_array, [(0, 0)] * (array.ndim - 1) + [(0, LANES - share)])

    weights = padded(jnp.transpose(input_proj, (1, 0, 2)))
    out_weights = output_proj
    if share != LANES:
        out_weights = jnp.pad(
            output_proj.reshape(ctx, share, cols), ((0, 0), (0, LANES - share), (0, 0))
        ).reshape(ctx * LANES, cols)
    own_filter = lax.dynamic_slice_in_dim(short_filter, me * filters, filters, 1)
    tap_rows = own_share(jnp.transpose(own_filter, (0, 2, 1)).reshape(branches * taps, filters))
    rate = lax.dynamic_slice_in_dim(pole_rate, me * filters, filters, 0)
    own_residue = lax.dynamic_slice_in_dim(residue, me * filters, filters, 0)
    amp = own_residue * jnp.sqrt(-jnp.expm1(-2.0 * rate))
    skip = lax.dynamic_slice_in_dim(skip_gain, me * share, share, 0)
    skip = jnp.pad(skip, (0, LANES - share)).reshape(1, LANES)

    vmem = pl.BlockSpec(memory_space=pltpu.VMEM)
    dma = pltpu.SemaphoreType.DMA
    wide_lanes = 3 * LANES
    result = pl.pallas_call(
        functools.partial(kernel, (groups, ctx, chans, ny, group_size)),
        out_shape=jax.ShapeDtypeStruct((genomes, local_len, cols * per), BF16),
        in_specs=[vmem] * 8 + [pl.BlockSpec(memory_space=pl.ANY)],
        out_specs=vmem,
        scratch_shapes=[
            pltpu.VMEM((ctx, genomes, local_len), jnp.int32),
            pltpu.VMEM((genomes, length, LANES), jnp.int32),
            pltpu.VMEM((nz, rows, wide_lanes), BF16),
            pltpu.VMEM((nz, rows, wide_lanes), F32),
            pltpu.VMEM((nz, rows, wide_lanes), BF16),
            pltpu.VMEM((nz, rows, wide_lanes), BF16),
            pltpu.VMEM((nz, rows, wide_lanes), BF16),
            pltpu.VMEM((nz, rows, wide_lanes), BF16),
            pltpu.VMEM((groups, rows, wide_lanes), BF16),
            pltpu.VMEM((filters, LANES, length), BF16),
            pltpu.VMEM((length, genomes * LANES), F32),
            pltpu.VMEM((ctx, genomes, length, LANES), BF16),
            pltpu.VMEM((genomes, length, cols), F32),
            pltpu.VMEM((genomes, half, cols), F32),
            pltpu.VMEM((genomes, half, cols), BF16),
            pltpu.VMEM((per, genomes, local_len, cols), BF16),
            pltpu.VMEM((vocab, cols), BF16),
            dma((ctx,)),
            dma((ctx,)),
            dma((nz,)),
            dma((nz,)),
            dma((nz,)),
            dma((nz,)),
            dma((nz,)),
            dma((groups,)),
            dma((groups,)),
            dma((ctx,)),
            dma((ctx,)),
            dma((ctx,)),
            dma((ctx,)),
            dma((1,)),
            dma((1,)),
            dma((per,)),
            dma((per,)),
            dma((1,)),
        ],
        compiler_params=pltpu.CompilerParams(
            collective_id=0, has_side_effects=True, vmem_limit_bytes=50 * 1024 * 1024
        ),
    )(
        tokens,
        normed,
        weights,
        tap_rows,
        rate[:, :, None],
        amp[:, :, None],
        skip,
        out_weights,
        embed_table,
    )
    return result


def solution(mesh):
    sizes = mesh.shape
    return jax.shard_map(
        functools.partial(body, sizes["groups"], sizes["ctx"], sizes["chan"]),
        mesh=mesh,
        in_specs=(
            P("groups", "ctx"),
            P(),
            P(),
            P("ctx", None, "chan"),
            P(None, "chan", None),
            P("chan", None),
            P("chan", None),
            P("chan"),
            P("chan", "ctx"),
        ),
        out_specs=P("groups", "ctx", "chan"),
        check_vma=False,
    )
```

time: 504 us -> 90.2 us (0.18)
  waiting for transfers between devices: 357 us -> 0 us
  Pallas kernels: 0 us -> 80.9 us
  matrix products: 46.2 us -> 0 us
  blocking collectives: 24.6 us -> 0 us
  local copies, waits for them, and re-layouts: 30 us -> 5.66 us
  other arithmetic: 21 us -> 3.27 us
  between operations: 13.3 us -> 0.03 us
  starting transfers between devices: 9.63 us -> 0 us
    reduce_scatter x2 -> x0, waiting for transfers between devices: 214 us -> none  [the longest x1 205 us: body(): lax.psum_scatter(jnp.dot(spread, flat_weight, preferred_element_type=jnp....]
    all_gather x2 -> x0, waiting for transfers between devices: 122 us -> none  [the longest x1 107 us: body(): lax.all_gather(output_proj, 'ctx', axis=1, tiled=True)]
    pallas_call x0 -> x1, Pallas kernels: none -> 80.9 us  [body(): pl.pallas_call(functools.partial(kernel, (groups, ctx, chans, ny, group_s...]
    dot_general x21 -> x0, matrix products: 46.2 us -> none  [the longest x8 11.9 us: local_block(): toeplitz = jnp.einsum('gnt,gns->gts', rising, falling, precision=highest)]
    all_gather x1 -> x0, blocking collectives: 24.6 us -> none  [entering(): everything = jax.tree.map(lambda part: lax.all_gather(part, axis), shard)]
    all_to_all x1 -> x0, waiting for transfers between devices: 19.9 us -> none  [body(): lax.all_to_all(normed, 'ctx', split_axis=1, concat_axis=0, tiled=True)]
    unnamed x20 -> x9, local copies, waits for them, and re-layouts: 13.9 us -> 2.83 us
    select_n x8 -> x0, other arithmetic: 9.29 us -> none  [hop(): return jax.tree.map(lambda a, b: jnp.where(reached, a, b), new, before)]
  transfers between devices with their start and end apart: 6 -> 0, of which waited for: 5 -> 0; matrix products, arithmetic and copies ran while one was open for 12% -> 0% of each run, Pallas kernels for 0% -> 0%
where the time goes in v1:
time: 90.2 us; the launch traced here: 89.8 us
  Pallas kernels  80.9 us (90%)
  local copies, waits for them, and re-layouts  5.66 us (6%)
  other arithmetic  3.27 us (4%)
    pallas_call x1, Pallas kernels, body(): pl.pallas_call(functools.partial(kernel, (groups, ctx, chans, ny, group_s...  80.9 us
    unnamed x9, local copies, waits for them, and re-layouts  2.83 us
    reduce_sum x1, other arithmetic, body(): inv_rms = lax.rsqrt(jnp.mean(wide * wide, axis=-1, keepdims=True) + EPSILON)  2.08 us

profile of v1, /device:TPU:1, one launch (start us, length us, event | category | flops | bytes accessed | tf_op | source)
XLA Modules:
  0.0 89.8 jit_solution(8884638674605354903)
XLA Ops:
  0.0 0.0 copy-start
  0.0 0.8 dynamic-slice_bitcast_fusion.1.skip_ref
  0.8 2.1 %multiply_reduce_fusion = f32[256]{0:T(256)S(1)} fusion(bf16[512,4096]{1,0:T(8,128)(2,1)} %table_ref.1, s32[]{:T(128)S(6)} %select_n.19), kind=kLoop, calls=%fused_computation | loop fusion | flops 3145472 | bytes 2098180 | tf_op jit(solution)/shard_map/reduce_sum | solution.py:485
  2.9 0.8 dynamic_slice.23
  3.6 0.0 copy-done
  3.6 0.1 dynamic-slice_bitcast_fusion
  3.7 0.8 constant_dynamic-slice_fusion
  4.5 0.1 copy.19
  4.6 0.1 copy.18
  4.7 0.1 broadcast_in_dim.11
  4.7 0.1 reshape.19.taps_ref
  4.8 0.1 copy.16.rate_ref
  5.0 0.1 copy.17.amp_ref
  5.1 1.2 %multiply_convert_fusion.norm_ref = bf16[256,512]{1,0:T(8,128)(2,1)S(1)} fusion(f32[512]{0:T(512)S(1)} %dynamic_slice.23, f32[256]{0:T(256)S(1)} %add_rsqrt_fusion, bf16[512,4096]{1,0:T(8,128)(2,1)} %table_ref.1, s32[]{:T(128)S(6)} %select_n.20, s32[]{:T(128)S(6)} %select_n.22), kind=kLoop, calls=%fused_computation.1 | loop fusion | flops 524288 | bytes 527368 | tf_op jit(solution)/shard_map/convert_element_type | solution.py:488
  6.2 0.0 copy-start.1
  6.3 1.2 %copy-done.1 = bf16[1024,512]{1,0:T(8,128)(2,1)S(1)} copy-done((bf16[1024,512]{1,0:T(8,128)(2,1)S(1)}, bf16[1024,512]{1,0:T(8,128)(2,1)}, u32[]{:S(2)}) %copy-start.1) | copy-done | bytes 1048600
  7.5 0.0 copy-start.2
  7.5 0.7 copy-done.2
  8.2 80.9 %shard_map.91 = bf16[2,64,2048]{2,1,0:T(8,128)(2,1)S(1)} custom-call(s32[2,64]{1,0:T(2,128)S(1)} %copy-done.2, bf16[256,512]{1,0:T(8,128)(2,1)S(1)} %multiply_convert_fusion.norm_ref, bf16[3,512,1024]{2,1,0:T(8,128)(2,1)} %bitcast.8, f32[9,128]{1,0:T(8,128)S(1)} %reshape.19.taps_ref, f32[8,16,1]{2,1,0:T(8,128)S(1)} %copy.16.rate_ref, ...), custom_call_target="tpu_custom_call" | custom-call | tf_op jit(solution)/shard_map/pallas_call | solution.py:518
  89.0 0.8 copy.21
  (3 shorter events, 0.0 us)
Async XLA Ops:
  0.0 3.6 %copy-start = (f32[3,64,3]{1,2,0:T(4,128)S(1)}, f32[3,64,3]{1,2,0:T(4,128)}, u32[]{:S(2)}) copy-start(f32[3,64,3]{1,2,0:T(4,128)} %param.13) | copy-start | bytes 6916
  6.2 1.2 %copy-start.1 = (bf16[1024,512]{1,0:T(8,128)(2,1)S(1)}, bf16[1024,512]{1,0:T(8,128)(2,1)}, u32[]{:S(2)}) copy-start(bf16[1024,512]{1,0:T(8,128)(2,1)} %wout_ref.1) | copy-start | bytes 3145732
  7.5 0.7 copy-start.2

commit v2 on v1

v2 whole, which is shorter than its diff:
```python
import functools

import jax
import jax.numpy as jnp
from jax import lax
from jax.experimental import pallas as pl
from jax.experimental.pallas import tpu as pltpu
from jax.sharding import PartitionSpec as P

EPSILON = 1e-06
LANES = 128
PIECES = 2
MESH = pl.DeviceIdType.MESH
F32 = jnp.float32
BF16 = jnp.bfloat16


def remote(src, dst, send_sem, recv_sem, where):
    return pltpu.make_async_remote_copy(
        src_ref=src,
        dst_ref=dst,
        send_sem=send_sem,
        recv_sem=recv_sem,
        device_id=where,
        device_id_type=MESH,
    )


def kernel(
    sizes,
    tok_ref,
    norm_ref,
    w_ref,
    taps_ref,
    rate_ref,
    amp_ref,
    skip_ref,
    wout_ref,
    table_ref,
    out_ref,
    tok_all,
    tok_col,
    part_y,
    part_own,
    recv_y,
    recv_r,
    recv_l,
    sum_z,
    vocab_proj,
    toeplitz,
    conv,
    gathered,
    acc,
    recv_c,
    obuf,
    land,
    table_cols,
    tok_send,
    tok_recv,
    ysend,
    yrecv,
    zsend,
    rrecv,
    lrecv,
    gsend,
    grecv,
    ar_send,
    al_send,
    ay_send,
    arecv,
    csend,
    crecv,
    osend,
    orecv,
    local_sem,
):
    groups, ctx, chans, ny, group_size = sizes
    nz = ctx // ny
    genomes, local_len = tok_ref.shape
    length = local_len * ctx
    rows = norm_ref.shape[0]
    vocab = rows * groups
    cols = wout_ref.shape[1]
    poles = rate_ref.shape[1]
    filters = rate_ref.shape[0]
    half = length // chans
    per = ctx // chans

    gi = lax.axis_index("groups")
    me = lax.axis_index("ctx")
    ci = lax.axis_index("chan")
    y = lax.rem(me, ny)
    z = me // ny
    other_y = z * ny + (ny - 1 - y)
    right, left = me + ny, me - ny
    dest_chan = me // per

    barrier = pltpu.get_barrier_semaphore()

    def greet(where):
        pl.semaphore_signal(barrier, inc=1, device_id=where, device_id_type=MESH)

    for off in range(1, ctx):
        greet({"ctx": lax.rem(me + off, ctx)})
    for off in range(1, groups):
        greet({"groups": lax.rem(gi + off, groups)})
    greet({"chan": 1 - ci})
    for q in range(per):
        target = ci * per + q

        @pl.when(jnp.logical_or(target != me, dest_chan != ci))
        def _():
            greet({"ctx": target, "chan": dest_chan})

    table_copy = pltpu.make_async_copy(
        table_ref.at[:, pl.ds(pl.multiple_of(me * cols, LANES), cols)], table_cols, local_sem.at[0]
    )
    table_copy.start()
    self_target = jnp.where(dest_chan == ci, 1, 0)
    pl.semaphore_wait(barrier, ctx - 1 + groups - 1 + 1 + per - self_target)

    tok_all[me] = tok_ref[...]
    for off in range(1, ctx):
        peer = lax.rem(me + off, ctx)
        remote(
            tok_ref, tok_all.at[me], tok_send.at[off], tok_recv.at[me], {"ctx": peer}
        ).start()

    pieces = part_own.shape[1]
    piece = rows // pieces

    def project(h, block, branch):
        columns = pl.ds(pl.multiple_of(block * LANES, LANES), LANES)
        return jnp.dot(
            norm_ref[h * piece : (h + 1) * piece, :],
            w_ref[branch, :, columns],
            preferred_element_type=F32,
        )

    order = []
    for step in range((nz + 1) // 2):
        order.append(nz - 1 - step)
        if step != nz - 1 - step:
            order.append(step)

    def y_copy(dz, h):
        return remote(
            part_y.at[dz, h], recv_y.at[dz, h], ysend.at[dz, h], yrecv.at[dz, h], {"ctx": other_y}
        )

    for h in range(pieces):
        if ny == 2:
            for dz in order:
                for branch in range(3):
                    part_y[dz, h, :, branch * LANES : (branch + 1) * LANES] = project(
                        h, dz * ny + 1 - y, branch
                    ).astype(BF16)
                y_copy(dz, h).start()
    for h in range(pieces):
        for dz in order:
            for branch in range(3):
                part_own[dz, h, :, branch * LANES : (branch + 1) * LANES] = project(
                    h, dz * ny + y, branch
                )

    def with_y(dz, h):
        value = part_own[dz, h]
        if ny == 2:
            y_copy(dz, h).wait_recv()
            value = value + recv_y[dz, h].astype(F32)
        return value

    def right_copy(dz, h):
        return remote(
            sum_z.at[dz, h], recv_r.at[dz, h], zsend.at[dz, h], rrecv.at[dz, h], {"ctx": right}
        )

    def left_copy(dz, h):
        return remote(
            sum_z.at[dz, h], recv_l.at[dz, h], zsend.at[dz, h], lrecv.at[dz, h], {"ctx": left}
        )

    def sum_step(h, step):
        dr, dl = nz - 1 - step, step

        @pl.when(z < dr)
        def _():
            part_own[dr, h] = with_y(dr, h)

            @pl.when(z > 0)
            def _():
                right_copy(dr, h).wait_recv()
                part_own[dr, h] = part_own[dr, h] + recv_r[dr, h].astype(F32)

            sum_z[dr, h] = part_own[dr, h].astype(BF16)
            right_copy(dr, h).start()

        @pl.when(z > dl)
        def _():
            part_own[dl, h] = with_y(dl, h)

            @pl.when(z < nz - 1)
            def _():
                left_copy(dl, h).wait_recv()
                part_own[dl, h] = part_own[dl, h] + recv_l[dl, h].astype(F32)

            sum_z[dl, h] = part_own[dl, h].astype(BF16)
            left_copy(dl, h).start()

    def group_copy(off, h, source, peer):
        return remote(
            vocab_proj.at[source, h],
            vocab_proj.at[source, h],
            gsend.at[off, h],
            grecv.at[source, h],
            {"groups": peer},
        )

    def finish(h):
        part_own[z, h] = with_y(z, h)

        @pl.when(z > 0)
        def _():
            right_copy(z, h).wait_recv()
            part_own[z, h] = part_own[z, h] + recv_r[z, h].astype(F32)

        @pl.when(z < nz - 1)
        def _():
            left_copy(z, h).wait_recv()
            part_own[z, h] = part_own[z, h] + recv_l[z, h].astype(F32)

        vocab_proj[gi, h] = part_own[z, h].astype(BF16)
        for off in range(1, groups):
            group_copy(off, h, gi, lax.rem(gi + off, groups)).start()

    width = length + LANES
    lag = length - 1 - lax.broadcasted_iota(jnp.int32, (poles, width), 1)
    lag_f = jnp.maximum(lag, 0).astype(F32)

    def long_filter(f):
        taps = jnp.sum(amp_ref[f] * jnp.exp(-rate_ref[f] * lag_f), axis=0, keepdims=True)
        taps = jnp.where(lag[:1] >= 0, taps, 0.0)
        rolled = pltpu.roll(
            jnp.broadcast_to(taps, (LANES, width)), width - (LANES - 1), 1, stride=1, stride_axis=0
        )
        toeplitz[f] = rolled[:, :length].astype(BF16)

    steps = []
    for h in range(pieces):
        for step in range(nz - 1):
            steps.append((sum_step, (h, step)))
            if step == 0 and h > 0:
                steps.append((finish, (h - 1,)))
    waiting = list(range(filters))
    for action, arguments in steps:
        action(*arguments)
        for f in waiting[:2]:
            long_filter(f)
        waiting = waiting[2:]
    for f in waiting:
        long_filter(f)

    for off in range(1, ctx):
        peer = lax.rem(me + off, ctx)
        remote(
            tok_ref, tok_all.at[peer], tok_send.at[off], tok_recv.at[peer], {"ctx": peer}
        ).wait_recv()
    for b in range(genomes):
        line = jnp.concatenate([tok_all[i, b : b + 1, :] for i in range(ctx)], axis=1)
        tok_col[b] = jnp.transpose(jnp.broadcast_to(line, (LANES, length)))

    finish(pieces - 1)
    for h in range(pieces):
        for off in range(1, groups):
            peer = lax.rem(gi + off, groups)
            group_copy(off, h, peer, peer).wait_recv()

    table_proj = vocab_proj[...].reshape(vocab, 3 * LANES)

    def onehot(columns):
        parts = []
        for v in range(vocab // LANES):
            ids = lax.broadcasted_iota(jnp.int32, columns.shape, 1) + v * LANES
            parts.append(jnp.where(columns == ids, 1.0, 0.0).astype(BF16))
        return jnp.concatenate(parts, axis=1)

    row_ids = lax.broadcasted_iota(jnp.int32, (length, LANES), 0)
    lane_filter = lax.broadcasted_iota(jnp.int32, (length, LANES), 1) // group_size
    blocks = length // LANES

    def along(slot, b, sems, where):
        return remote(
            gathered.at[slot, b],
            gathered.at[slot, b],
            sems.at[slot, b],
            arecv.at[slot, b],
            {"ctx": where},
        )

    for b in range(genomes):
        projected = jnp.dot(onehot(tok_col[b]), table_proj, preferred_element_type=F32)
        filtered = []
        for branch in range(3):
            value = projected[:, branch * LANES : (branch + 1) * LANES]
            total = taps_ref[branch * 3 : branch * 3 + 1, :] * value
            for k in (1, 2):
                shifted = jnp.where(row_ids >= k, pltpu.roll(value, k, 0), 0.0)
                at = branch * 3 + k
                total = total + taps_ref[at : at + 1, :] * shifted
            filtered.append(total)
        product = filtered[1] * filtered[2]
        for f in range(filters):
            masked = jnp.where(lane_filter == f, product, 0.0).astype(BF16)
            for i in range(blocks):
                term = jnp.dot(
                    toeplitz[f, :, (blocks - 1 - i) * LANES :],
                    masked[: (i + 1) * LANES],
                    preferred_element_type=F32,
                )
                at = slice(i * LANES, (i + 1) * LANES)
                conv[at, :] = term if f == 0 else conv[at, :] + term
        gated = filtered[0] * (conv[...] + skip_ref[...] * product)
        gathered[me, b] = gated.astype(BF16)

        @pl.when(z < nz - 1)
        def _():
            along(me, b, ar_send, right).start()

        @pl.when(z > 0)
        def _():
            along(me, b, al_send, left).start()

        if ny == 2:
            along(me, b, ay_send, other_y).start()

    def block_product(slot, b):
        weight = wout_ref[pl.ds(pl.multiple_of(slot * LANES, LANES), LANES), :]
        return jnp.dot(gathered[slot, b], weight, preferred_element_type=F32)

    mine = pl.ds(pl.multiple_of(ci * half, LANES), half)
    table_copy.wait()
    for b in range(genomes):
        acc[b] = block_product(me, b)
        acc[b, mine, :] = acc[b, mine, :] + jnp.dot(
            onehot(tok_col[b, mine, :]), table_cols[...], preferred_element_type=F32
        )

    def multiply(slot, b):
        acc[b] = acc[b] + block_product(slot, b)

    def z_step(b, step):
        from_left = me - step * ny
        from_right = me + step * ny

        @pl.when(from_left >= 0)
        def _():
            along(from_left, b, ar_send, right).wait_recv()

            @pl.when(z < nz - 1)
            def _():
                along(from_left, b, ar_send, right).start()

            if ny == 2:
                along(from_left, b, ay_send, other_y).start()

        @pl.when(from_right < ctx)
        def _():
            along(from_right, b, al_send, left).wait_recv()

            @pl.when(z > 0)
            def _():
                along(from_right, b, al_send, left).start()

            if ny == 2:
                along(from_right, b, ay_send, other_y).start()

        @pl.when(from_left >= 0)
        def _():
            multiply(from_left, b)

        @pl.when(from_right < ctx)
        def _():
            multiply(from_right, b)

    def y_step(b):
        if ny == 1:
            return
        for step in range(nz):
            for toward in (-1, 1) if step > 0 else (1,):
                twin_z = z + toward * step

                @pl.when(jnp.logical_and(twin_z >= 0, twin_z < nz))
                def _():
                    slot = twin_z * ny + (1 - y)
                    along(slot, b, ay_send, other_y).wait_recv()
                    multiply(slot, b)

    def swap(b):
        return remote(
            acc.at[b, pl.ds(pl.multiple_of((1 - ci) * half, LANES), half), :],
            recv_c.at[b],
            csend.at[b],
            crecv.at[b],
            {"chan": 1 - ci},
        )

    def out_copy(q, b, source_slot):
        return remote(
            obuf.at[b, pl.ds(q * local_len, local_len), :],
            land.at[source_slot, b],
            osend.at[q, b],
            orecv.at[source_slot, b],
            {"ctx": ci * per + q, "chan": dest_chan},
        )

    def is_self(q):
        return jnp.logical_and(ci * per + q == me, dest_chan == ci)

    my_slot = lax.rem(me, per)

    def send_out(b):
        swap(b).wait()
        obuf[b] = (acc[b, mine, :] + recv_c[b]).astype(BF16)
        for q in range(per):

            @pl.when(jnp.logical_not(is_self(q)))
            def _():
                out_copy(q, b, my_slot).start()

            @pl.when(is_self(q))
            def _():
                land[my_slot, b] = obuf[b, q * local_len : (q + 1) * local_len, :]

    for b in range(genomes):
        for step in range(1, nz):
            if b == 0 or step == nz - 1:
                z_step(b, step)
            if step >= 2 and b + 1 < genomes:
                z_step(b + 1, step - 1)
        if b > 0:
            send_out(b - 1)
        y_step(b)
        swap(b).start()
    send_out(genomes - 1)

    for b in range(genomes):
        for q in range(per):

            @pl.when(jnp.logical_not(is_self(q)))
            def _():
                out_copy(q, b, q).wait_recv()

            out_ref[b, :, q * cols : (q + 1) * cols] = land[q, b]

    for off in range(1, ctx):
        remote(
            tok_ref, tok_all.at[me], tok_send.at[off], tok_recv.at[me], {"ctx": lax.rem(me + off, ctx)}
        ).wait_send()
    for h in range(pieces):
        for off in range(1, groups):
            group_copy(off, h, gi, lax.rem(gi + off, groups)).wait_send()
        for dz in range(nz):
            if ny == 2:
                y_copy(dz, h).wait_send()

            @pl.when(z < dz)
            def _():
                right_copy(dz, h).wait_send()

            @pl.when(z > dz)
            def _():
                left_copy(dz, h).wait_send()

    for b in range(genomes):
        for q in range(per):

            @pl.when(jnp.logical_not(is_self(q)))
            def _():
                out_copy(q, b, my_slot).wait_send()

        for dz in range(nz):
            slot = dz * ny + y

            @pl.when(jnp.logical_and(dz <= z, z < nz - 1))
            def _():
                along(slot, b, ar_send, right).wait_send()

            @pl.when(jnp.logical_and(dz >= z, z > 0))
            def _():
                along(slot, b, al_send, left).wait_send()

            if ny == 2:
                along(slot, b, ay_send, other_y).wait_send()


def body(
    groups,
    ctx,
    chans,
    tokens,
    embed_table,
    norm_gain,
    input_proj,
    short_filter,
    pole_rate,
    residue,
    skip_gain,
    output_proj,
):
    genomes, local_len = tokens.shape
    length = local_len * ctx
    features, branches, channels = input_proj.shape
    vocab = embed_table.shape[0]
    filter_count, poles = pole_rate.shape
    group_size = channels // filter_count
    share = channels // ctx
    filters = filter_count // ctx
    cols = output_proj.shape[1]
    rows = vocab // groups
    ny = 2 if ctx % 2 == 0 and ctx <= 8 else 1
    nz = ctx // ny
    taps = short_filter.shape[2]
    me = lax.axis_index("ctx")
    gi = lax.axis_index("groups")
    half = length // chans
    per = ctx // chans

    own_rows = lax.dynamic_slice_in_dim(embed_table, gi * rows, rows, 0)
    wide = own_rows.astype(F32)
    inv_rms = lax.rsqrt(jnp.mean(wide * wide, axis=-1, keepdims=True) + EPSILON)
    own_feats = lax.dynamic_slice_in_dim(own_rows, me * features, features, 1).astype(F32)
    gain = lax.dynamic_slice_in_dim(norm_gain, me * features, features, 0)
    normed = (own_feats * inv_rms * gain).astype(BF16)

    def padded(array):
        if share == LANES:
            return array
        cut = array.reshape(array.shape[:-1] + (ctx, share))
        pads = [(0, 0)] * (cut.ndim - 1) + [(0, LANES - share)]
        return jnp.pad(cut, pads).reshape(array.shape[:-1] + (ctx * LANES,))

    def own_share(array):
        wide_array = jnp.repeat(array, group_size, axis=-1)
        return jnp.pad(wide_array, [(0, 0)] * (array.ndim - 1) + [(0, LANES - share)])

    weights = padded(jnp.transpose(input_proj, (1, 0, 2)))
    out_weights = output_proj
    if share != LANES:
        out_weights = jnp.pad(
            output_proj.reshape(ctx, share, cols), ((0, 0), (0, LANES - share), (0, 0))
        ).reshape(ctx * LANES, cols)
    own_filter = lax.dynamic_slice_in_dim(short_filter, me * filters, filters, 1)
    tap_rows = own_share(jnp.transpose(own_filter, (0, 2, 1)).reshape(branches * taps, filters))
    rate = lax.dynamic_slice_in_dim(pole_rate, me * filters, filters, 0)
    own_residue = lax.dynamic_slice_in_dim(residue, me * filters, filters, 0)
    amp = own_residue * jnp.sqrt(-jnp.expm1(-2.0 * rate))
    skip = lax.dynamic_slice_in_dim(skip_gain, me * share, share, 0)
    skip = jnp.pad(skip, (0, LANES - share)).reshape(1, LANES)

    vmem = pl.BlockSpec(memory_space=pltpu.VMEM)
    dma = pltpu.SemaphoreType.DMA
    wide_lanes = 3 * LANES
    result = pl.pallas_call(
        functools.partial(kernel, (groups, ctx, chans, ny, group_size)),
        out_shape=jax.ShapeDtypeStruct((genomes, local_len, cols * per), BF16),
        in_specs=[vmem] * 8 + [pl.BlockSpec(memory_space=pl.ANY)],
        out_specs=vmem,
        scratch_shapes=[
            pltpu.VMEM((ctx, genomes, local_len), jnp.int32),
            pltpu.VMEM((genomes, length, LANES), jnp.int32),
            pltpu.VMEM((nz, PIECES, rows // PIECES, wide_lanes), BF16),
            pltpu.VMEM((nz, PIECES, rows // PIECES, wide_lanes), F32),
            pltpu.VMEM((nz, PIECES, rows // PIECES, wide_lanes), BF16),
            pltpu.VMEM((nz, PIECES, rows // PIECES, wide_lanes), BF16),
            pltpu.VMEM((nz, PIECES, rows // PIECES, wide_lanes), BF16),
            pltpu.VMEM((nz, PIECES, rows // PIECES, wide_lanes), BF16),
            pltpu.VMEM((groups, PIECES, rows // PIECES, wide_lanes), BF16),
            pltpu.VMEM((filters, LANES, length), BF16),
            pltpu.VMEM((length, LANES), F32),
            pltpu.VMEM((ctx, genomes, length, LANES), BF16),
            pltpu.VMEM((genomes, length, cols), F32),
            pltpu.VMEM((genomes, half, cols), F32),
            pltpu.VMEM((genomes, half, cols), BF16),
            pltpu.VMEM((per, genomes, local_len, cols), BF16),
            pltpu.VMEM((vocab, cols), BF16),
            dma((ctx,)),
            dma((ctx,)),
            dma((nz, PIECES)),
            dma((nz, PIECES)),
            dma((nz, PIECES)),
            dma((nz, PIECES)),
            dma((nz, PIECES)),
            dma((groups, PIECES)),
            dma((groups, PIECES)),
            dma((ctx, genomes)),
            dma((ctx, genomes)),
            dma((ctx, genomes)),
            dma((ctx, genomes)),
            dma((genomes,)),
            dma((genomes,)),
            dma((per, genomes)),
            dma((per, genomes)),
            dma((1,)),
        ],
        compiler_params=pltpu.CompilerParams(
            collective_id=0, has_side_effects=True, vmem_limit_bytes=50 * 1024 * 1024
        ),
    )(
        tokens,
        normed,
        weights,
        tap_rows,
        rate[:, :, None],
        amp[:, :, None],
        skip,
        out_weights,
        embed_table,
    )
    return result


def solution(mesh):
    sizes = mesh.shape
    return jax.shard_map(
        functools.partial(body, sizes["groups"], sizes["ctx"], sizes["chan"]),
        mesh=mesh,
        in_specs=(
            P("groups", "ctx"),
            P(),
            P(),
            P("ctx", None, "chan"),
            P(None, "chan", None),
            P("chan", None),
            P("chan", None),
            P("chan"),
            P("chan", "ctx"),
        ),
        out_specs=P("groups", "ctx", "chan"),
        check_vma=False,
    )
```

time: 90.2 us -> 84.3 us (0.935)
  Pallas kernels: 80.9 us -> 75 us
    pallas_call x1, Pallas kernels: 80.9 us -> 75 us  [body(): pl.pallas_call(functools.partial(kernel, (groups, ctx, chans, ny, group_s...]
where the time goes in v2:
time: 84.3 us; the launch traced here: 83.9 us
  Pallas kernels  75 us (89%)
  local copies, waits for them, and re-layouts  5.66 us (7%)
  other arithmetic  3.27 us (4%)
    pallas_call x1, Pallas kernels, body(): pl.pallas_call(functools.partial(kernel, (groups, ctx, chans, ny, group_s...  75 us
    unnamed x9, local copies, waits for them, and re-layouts  2.83 us
    reduce_sum x1, other arithmetic, body(): inv_rms = lax.rsqrt(jnp.mean(wide * wide, axis=-1, keepdims=True) + EPSILON)  2.08 us

profile of v2, /device:TPU:1, one launch (start us, length us, event | category | flops | bytes accessed | tf_op | source)
XLA Modules:
  0.0 83.9 jit_solution(1666748970829279862)
XLA Ops:
  0.0 0.0 copy-start
  0.0 0.8 dynamic-slice_bitcast_fusion.1.skip_ref
  0.8 2.1 %multiply_reduce_fusion = f32[256]{0:T(256)S(1)} fusion(bf16[512,4096]{1,0:T(8,128)(2,1)} %table_ref.1, s32[]{:T(128)S(6)} %select_n.19), kind=kLoop, calls=%fused_computation | loop fusion | flops 3145472 | bytes 2098180 | tf_op jit(solution)/shard_map/reduce_sum | solution.py:530
  2.9 0.8 dynamic_slice.23
  3.6 0.0 copy-done
  3.6 0.1 dynamic-slice_bitcast_fusion
  3.7 0.8 constant_dynamic-slice_fusion
  4.5 0.1 copy.19
  4.6 0.1 copy.18
  4.7 0.1 broadcast_in_dim.11
  4.7 0.1 reshape.19.taps_ref
  4.8 0.1 copy.16.rate_ref
  5.0 0.1 copy.17.amp_ref
  5.1 1.2 %multiply_convert_fusion.norm_ref = bf16[256,512]{1,0:T(8,128)(2,1)S(1)} fusion(f32[512]{0:T(512)S(1)} %dynamic_slice.23, f32[256]{0:T(256)S(1)} %add_rsqrt_fusion, bf16[512,4096]{1,0:T(8,128)(2,1)} %table_ref.1, s32[]{:T(128)S(6)} %select_n.20, s32[]{:T(128)S(6)} %select_n.22), kind=kLoop, calls=%fused_computation.1 | loop fusion | flops 524288 | bytes 527368 | tf_op jit(solution)/shard_map/convert_element_type | solution.py:533
  6.2 0.0 copy-start.1
  6.3 1.2 %copy-done.1 = bf16[1024,512]{1,0:T(8,128)(2,1)S(1)} copy-done((bf16[1024,512]{1,0:T(8,128)(2,1)S(1)}, bf16[1024,512]{1,0:T(8,128)(2,1)}, u32[]{:S(2)}) %copy-start.1) | copy-done | bytes 1048600
  7.5 0.0 copy-start.2
  7.5 0.7 copy-done.2
  8.2 75.0 %shard_map.91 = bf16[2,64,2048]{2,1,0:T(8,128)(2,1)S(1)} custom-call(s32[2,64]{1,0:T(2,128)S(1)} %copy-done.2, bf16[256,512]{1,0:T(8,128)(2,1)S(1)} %multiply_convert_fusion.norm_ref, bf16[3,512,1024]{2,1,0:T(8,128)(2,1)} %bitcast.8, f32[9,128]{1,0:T(8,128)S(1)} %reshape.19.taps_ref, f32[8,16,1]{2,1,0:T(8,128)S(1)} %copy.16.rate_ref, ...), custom_call_target="tpu_custom_call" | custom-call | tf_op jit(solution)/shard_map/pallas_call | solution.py:563
  83.1 0.8 copy.21
  (3 shorter events, 0.0 us)
Async XLA Ops:
  0.0 3.6 %copy-start = (f32[3,64,3]{1,2,0:T(4,128)S(1)}, f32[3,64,3]{1,2,0:T(4,128)}, u32[]{:S(2)}) copy-start(f32[3,64,3]{1,2,0:T(4,128)} %param.13) | copy-start | bytes 6916
  6.2 1.2 %copy-start.1 = (bf16[1024,512]{1,0:T(8,128)(2,1)S(1)}, bf16[1024,512]{1,0:T(8,128)(2,1)}, u32[]{:S(2)}) copy-start(bf16[1024,512]{1,0:T(8,128)(2,1)} %wout_ref.1) | copy-start | bytes 3145732
  7.5 0.7 copy-start.2

commit v3 on v2

--- a/solution.py
+++ b/solution.py
@@ -9,7 +9,7 @@
 
 EPSILON = 1e-06
 LANES = 128
-PIECES = 2
+PIECES = 4
 MESH = pl.DeviceIdType.MESH
 F32 = jnp.float32
 BF16 = jnp.bfloat16
@@ -28,16 +28,27 @@
 
 def kernel(
     sizes,
+    tok_hbm,
+    gain_hbm,
+    w_hbm,
+    taps_hbm,
+    rate_hbm,
+    residue_hbm,
+    skip_hbm,
+    wout_hbm,
+    table_ref,
+    out_ref,
     tok_ref,
-    norm_ref,
+    gain_ref,
     w_ref,
-    taps_ref,
+    short_ref,
     rate_ref,
-    amp_ref,
+    residue_ref,
     skip_ref,
     wout_ref,
-    table_ref,
-    out_ref,
+    own_rows,
+    norm_ref,
+    taps_ref,
     tok_all,
     tok_col,
     part_y,
@@ -74,15 +85,15 @@
     orecv,
     local_sem,
 ):
-    groups, ctx, chans, ny, group_size = sizes
+    groups, ctx, chans, ny, group_size, filters = sizes
     nz = ctx // ny
     genomes, local_len = tok_ref.shape
     length = local_len * ctx
-    rows = norm_ref.shape[0]
+    rows, features = norm_ref.shape
+    width_all = own_rows.shape[1]
     vocab = rows * groups
     cols = wout_ref.shape[1]
-    poles = rate_ref.shape[1]
-    filters = rate_ref.shape[0]
+    poles, filters_all = rate_ref.shape
     half = length // chans
     per = ctx // chans
 
@@ -112,10 +123,40 @@
         def _():
             greet({"ctx": target, "chan": dest_chan})
 
-    table_copy = pltpu.make_async_copy(
-        table_ref.at[:, pl.ds(pl.multiple_of(me * cols, LANES), cols)], table_cols, local_sem.at[0]
-    )
-    table_copy.start()
+    def lane_block(ref, index, size):
+        return ref.at[:, pl.ds(pl.multiple_of(index * size, LANES), size)]
+
+    loads = [
+        (table_ref.at[pl.ds(pl.multiple_of(gi * rows, 16), rows), :], own_rows),
+        (lane_block(gain_hbm, me, features), gain_ref),
+        (w_hbm, w_ref),
+        (tok_hbm, tok_ref),
+        (taps_hbm, short_ref),
+        (rate_hbm, rate_ref),
+        (residue_hbm, residue_ref),
+        (lane_block(skip_hbm, me, LANES), skip_ref),
+        (wout_hbm, wout_ref),
+        (lane_block(table_ref, me, cols), table_cols),
+    ]
+    copies = [
+        pltpu.make_async_copy(source, target, local_sem.at[n])
+        for n, (source, target) in enumerate(loads)
+    ]
+    for copy in copies:
+        copy.start()
+
+    copies[0].wait()
+    copies[1].wait()
+    squares = jnp.zeros((rows, LANES), F32)
+    for at in range(0, width_all, LANES):
+        wide = own_rows[:, at : at + LANES].astype(F32)
+        squares = squares + wide * wide
+    inv_rms = lax.rsqrt(jnp.sum(squares, axis=1, keepdims=True) / width_all + EPSILON)
+    feats = own_rows[:, pl.ds(pl.multiple_of(me * features, LANES), features)].astype(F32)
+    norm_ref[...] = (feats * inv_rms * gain_ref[...]).astype(BF16)
+    copies[3].wait()
+    copies[2].wait()
+
     self_target = jnp.where(dest_chan == ci, 1, 0)
     pl.semaphore_wait(barrier, ctx - 1 + groups - 1 + 1 + per - self_target)
 
@@ -129,14 +170,6 @@
     pieces = part_own.shape[1]
     piece = rows // pieces
 
-    def project(h, block, branch):
-        columns = pl.ds(pl.multiple_of(block * LANES, LANES), LANES)
-        return jnp.dot(
-            norm_ref[h * piece : (h + 1) * piece, :],
-            w_ref[branch, :, columns],
-            preferred_element_type=F32,
-        )
-
     order = []
     for step in range((nz + 1) // 2):
         order.append(nz - 1 - step)
@@ -148,20 +181,29 @@
             part_y.at[dz, h], recv_y.at[dz, h], ysend.at[dz, h], yrecv.at[dz, h], {"ctx": other_y}
         )
 
-    for h in range(pieces):
+    for dz in order:
+        for branch in range(3):
+            lanes = slice(branch * LANES, (branch + 1) * LANES)
+            both = jnp.dot(
+                norm_ref[...],
+                w_ref[branch, :, dz * ny * LANES : (dz + 1) * ny * LANES],
+                preferred_element_type=F32,
+            )
+            keep = both
+            if ny == 2:
+                first, second = both[:, :LANES], both[:, LANES:]
+                keep = jnp.where(y == 0, first, second)
+                give = jnp.where(y == 0, second, first).astype(BF16)
+            for h in range(pieces):
+                part_own[dz, h, :, lanes] = keep[h * piece : (h + 1) * piece]
+                if ny == 2:
+                    part_y[dz, h, :, lanes] = give[h * piece : (h + 1) * piece]
         if ny == 2:
+            y_copy(dz, 0).start()
+    if ny == 2:
+        for h in range(1, pieces):
             for dz in order:
-                for branch in range(3):
-                    part_y[dz, h, :, branch * LANES : (branch + 1) * LANES] = project(
-                        h, dz * ny + 1 - y, branch
-                    ).astype(BF16)
                 y_copy(dz, h).start()
-    for h in range(pieces):
-        for dz in order:
-            for branch in range(3):
-                part_own[dz, h, :, branch * LANES : (branch + 1) * LANES] = project(
-                    h, dz * ny + y, branch
-                )
 
     def with_y(dz, h):
         value = part_own[dz, h]
@@ -237,8 +279,29 @@
     lag = length - 1 - lax.broadcasted_iota(jnp.int32, (poles, width), 1)
     lag_f = jnp.maximum(lag, 0).astype(F32)
 
+    for copy in copies[4:8]:
+        copy.wait()
+    doubled = -2.0 * rate_ref[...]
+    decayed = jnp.exp(doubled)
+    pole_amp = residue_ref[...] * jnp.sqrt((1.0 - decayed) * doubled / jnp.log(decayed))
+    filter_ids = lax.broadcasted_iota(jnp.int32, (poles, filters_all), 1)
+    lane_ids = lax.broadcasted_iota(jnp.int32, (filters_all, LANES), 1)
+    spread_ids = lane_ids // group_size
+    chosen = jnp.logical_and(
+        spread_ids < filters,
+        spread_ids + me * filters == lax.broadcasted_iota(jnp.int32, (filters_all, LANES), 0),
+    )
+    spread = jnp.where(chosen, 1.0, 0.0)
+    for branch in range(3):
+        taps_ref[branch * 3 : (branch + 1) * 3, :] = jnp.dot(
+            short_ref[branch], spread, precision=lax.Precision.HIGHEST, preferred_element_type=F32
+        )
+
     def long_filter(f):
-        taps = jnp.sum(amp_ref[f] * jnp.exp(-rate_ref[f] * lag_f), axis=0, keepdims=True)
+        here = filter_ids == me * filters + f
+        rate = jnp.sum(jnp.where(here, rate_ref[...], 0.0), axis=1, keepdims=True)
+        amp = jnp.sum(jnp.where(here, pole_amp, 0.0), axis=1, keepdims=True)
+        taps = jnp.sum(amp * jnp.exp(-rate * lag_f), axis=0, keepdims=True)
         taps = jnp.where(lag[:1] >= 0, taps, 0.0)
         rolled = pltpu.roll(
             jnp.broadcast_to(taps, (LANES, width)), width - (LANES - 1), 1, stride=1, stride_axis=0
@@ -338,7 +401,8 @@
         return jnp.dot(gathered[slot, b], weight, preferred_element_type=F32)
 
     mine = pl.ds(pl.multiple_of(ci * half, LANES), half)
-    table_copy.wait()
+    copies[8].wait()
+    copies[9].wait()
     for b in range(genomes):
         acc[b] = block_product(me, b)
         acc[b, mine, :] = acc[b, mine, :] + jnp.dot(
@@ -520,17 +584,8 @@
     ny = 2 if ctx % 2 == 0 and ctx <= 8 else 1
     nz = ctx // ny
     taps = short_filter.shape[2]
-    me = lax.axis_index("ctx")
-    gi = lax.axis_index("groups")
     half = length // chans
     per = ctx // chans
-
-    own_rows = lax.dynamic_slice_in_dim(embed_table, gi * rows, rows, 0)
-    wide = own_rows.astype(F32)
-    inv_rms = lax.rsqrt(jnp.mean(wide * wide, axis=-1, keepdims=True) + EPSILON)
-    own_feats = lax.dynamic_slice_in_dim(own_rows, me * features, features, 1).astype(F32)
-    gain = lax.dynamic_slice_in_dim(norm_gain, me * features, features, 0)
-    normed = (own_feats * inv_rms * gain).astype(BF16)
 
     def padded(array):
         if share == LANES:
@@ -539,33 +594,35 @@
         pads = [(0, 0)] * (cut.ndim - 1) + [(0, LANES - share)]
         return jnp.pad(cut, pads).reshape(array.shape[:-1] + (ctx * LANES,))
 
-    def own_share(array):
-        wide_array = jnp.repeat(array, group_size, axis=-1)
-        return jnp.pad(wide_array, [(0, 0)] * (array.ndim - 1) + [(0, LANES - share)])
-
     weights = padded(jnp.transpose(input_proj, (1, 0, 2)))
     out_weights = output_proj
     if share != LANES:
         out_weights = jnp.pad(
             output_proj.reshape(ctx, share, cols), ((0, 0), (0, LANES - share), (0, 0))
         ).reshape(ctx * LANES, cols)
-    own_filter = lax.dynamic_slice_in_dim(short_filter, me * filters, filters, 1)
-    tap_rows = own_share(jnp.transpose(own_filter, (0, 2, 1)).reshape(branches * taps, filters))
-    rate = lax.dynamic_slice_in_dim(pole_rate, me * filters, filters, 0)
-    own_residue = lax.dynamic_slice_in_dim(residue, me * filters, filters, 0)
-    amp = own_residue * jnp.sqrt(-jnp.expm1(-2.0 * rate))
-    skip = lax.dynamic_slice_in_dim(skip_gain, me * share, share, 0)
-    skip = jnp.pad(skip, (0, LANES - share)).reshape(1, LANES)
+    short = jnp.transpose(short_filter, (0, 2, 1))
+    skip = padded(skip_gain).reshape(1, ctx * LANES)
 
     vmem = pl.BlockSpec(memory_space=pltpu.VMEM)
     dma = pltpu.SemaphoreType.DMA
     wide_lanes = 3 * LANES
     result = pl.pallas_call(
-        functools.partial(kernel, (groups, ctx, chans, ny, group_size)),
+        functools.partial(kernel, (groups, ctx, chans, ny, group_size, filters)),
         out_shape=jax.ShapeDtypeStruct((genomes, local_len, cols * per), BF16),
-        in_specs=[vmem] * 8 + [pl.BlockSpec(memory_space=pl.ANY)],
+        in_specs=[pl.BlockSpec(memory_space=pl.ANY)] * 9,
         out_specs=vmem,
         scratch_shapes=[
+            pltpu.VMEM((genomes, local_len), jnp.int32),
+            pltpu.VMEM((1, features), F32),
+            pltpu.VMEM((branches, features, ctx * LANES), BF16),
+            pltpu.VMEM((branches, taps, filter_count), F32),
+            pltpu.VMEM((poles, filter_count), F32),
+            pltpu.VMEM((poles, filter_count), F32),
+            pltpu.VMEM((1, LANES), F32),
+            pltpu.VMEM((ctx * LANES, cols), BF16),
+            pltpu.VMEM((rows, features * ctx), BF16),
+            pltpu.VMEM((rows, features), BF16),
+            pltpu.VMEM((branches * taps, LANES), F32),
             pltpu.VMEM((ctx, genomes, local_len), jnp.int32),
             pltpu.VMEM((genomes, length, LANES), jnp.int32),
             pltpu.VMEM((nz, PIECES, rows // PIECES, wide_lanes), BF16),
@@ -600,18 +657,18 @@
             dma((genomes,)),
             dma((per, genomes)),
             dma((per, genomes)),
-            dma((1,)),
+            dma((10,)),
         ],
         compiler_params=pltpu.CompilerParams(
-            collective_id=0, has_side_effects=True, vmem_limit_bytes=50 * 1024 * 1024
+            collective_id=0, has_side_effects=True, vmem_limit_bytes=56 * 1024 * 1024
         ),
     )(
         tokens,
-        normed,
+        norm_gain.reshape(1, features * ctx),
         weights,
-        tap_rows,
-        rate[:, :, None],
-        amp[:, :, None],
+        short,
+        jnp.transpose(pole_rate),
+        jnp.transpose(residue),
         skip,
         out_weights,
         embed_table,

time: 84.3 us -> 82.6 us (0.980)
  Pallas kernels: 75 us -> 80.5 us
  local copies, waits for them, and re-layouts: 5.66 us -> 1.88 us
  other arithmetic: 3.27 us -> 0 us
    pallas_call x1, Pallas kernels: 75 us -> 80.5 us  [body(): pl.pallas_call(functools.partial(kernel, (groups, ctx, chans, ny, group_s...]
    reduce_sum x1 -> x0, other arithmetic: 2.08 us -> none  [body(): inv_rms = lax.rsqrt(jnp.mean(wide * wide, axis=-1, keepdims=True) + EPSILON)]
    dynamic_slice x2 -> x0, local copies, waits for them, and re-layouts: 1.55 us -> none  [the longest x1 0.79 us: body(): own_residue = lax.dynamic_slice_in_dim(residue, me * filters, filters, 0)]
    convert_element_type x1 -> x0, other arithmetic: 1.16 us -> none  [body(): normed = (own_feats * inv_rms * gain).astype(BF16)]
    unnamed x9 -> x1, local copies, waits for them, and re-layouts: 2.83 us -> 1.88 us
    reshape x3 -> x0, local copies, waits for them, and re-layouts: 0.87 us -> none  [the longest x1 0.77 us: body(): skip = jnp.pad(skip, (0, LANES - share)).reshape(1, LANES)]
where the time goes in v3:
time: 82.6 us; the launch traced here: 82.4 us
  Pallas kernels  80.5 us (97%)
  local copies, waits for them, and re-layouts  1.88 us (2%)
    pallas_call x1, Pallas kernels, body(): pl.pallas_call(functools.partial(kernel, (groups, ctx, chans, ny, group_s...  80.5 us
    unnamed x1, local copies, waits for them, and re-layouts  1.88 us

profile of v3, /device:TPU:1, one launch (start us, length us, event | category | flops | bytes accessed | tf_op | source)
XLA Modules:
  0.0 82.4 jit_solution(18239406749027327825)
XLA Ops:
  0.0 80.5 %shard_map.91 = bf16[2,64,2048]{2,1,0:T(8,128)(2,1)} custom-call(s32[2,64]{1,0:T(2,128)} %tok_hbm.1, f32[1,4096]{1,0:T(1,128)} %bitcast.7, bf16[3,512,1024]{2,1,0:T(8,128)(2,1)} %bitcast.6, f32[3,3,64]{2,1,0:T(4,128)} %bitcast.10, f32[16,64]{1,0:T(8,128)} %bitcast.8, f32[16,64]{1,0:T(8,128)} %bitcast.9, f32[1,1024]{1,0:T(1,128)} %bitcast.11, ...), custom_call_target="tpu_custom_call" | custom-call | tf_op jit(solution)/shard_map/pallas_call | solution.py:609
  80.5 1.9 %copy.11 = bf16[2,64,2048]{2,1,0:T(8,128)(2,1)} copy(bf16[2,64,2048]{2,1,0:T(8,128)(2,1)} %shard_map.91) | data formatting | bytes 1048576

commit v4 on v3

--- a/solution.py
+++ b/solution.py
@@ -9,7 +9,7 @@
 
 EPSILON = 1e-06
 LANES = 128
-PIECES = 4
+PIECES = 2
 MESH = pl.DeviceIdType.MESH
 F32 = jnp.float32
 BF16 = jnp.bfloat16

time: 82.6 us -> 76.4 us (0.925)
  Pallas kernels: 80.5 us -> 74.4 us
    pallas_call x1, Pallas kernels: 80.5 us -> 74.4 us  [body(): pl.pallas_call(functools.partial(kernel, (groups, ctx, chans, ny, group_s...]
where the time goes in v4:
time: 76.4 us; the launch traced here: 76.3 us
  Pallas kernels  74.4 us (97%)
  local copies, waits for them, and re-layouts  1.88 us (2%)
    pallas_call x1, Pallas kernels, body(): pl.pallas_call(functools.partial(kernel, (groups, ctx, chans, ny, group_s...  74.4 us
    unnamed x1, local copies, waits for them, and re-layouts  1.88 us

profile of v4, /device:TPU:1, one launch (start us, length us, event | category | flops | bytes accessed | tf_op | source)
XLA Modules:
  0.0 76.3 jit_solution(7143499446946508821)
XLA Ops:
  0.0 74.4 %shard_map.91 = bf16[2,64,2048]{2,1,0:T(8,128)(2,1)} custom-call(s32[2,64]{1,0:T(2,128)} %tok_hbm.1, f32[1,4096]{1,0:T(1,128)} %bitcast.7, bf16[3,512,1024]{2,1,0:T(8,128)(2,1)} %bitcast.6, f32[3,3,64]{2,1,0:T(4,128)} %bitcast.10, f32[16,64]{1,0:T(8,128)} %bitcast.8, f32[16,64]{1,0:T(8,128)} %bitcast.9, f32[1,1024]{1,0:T(1,128)} %bitcast.11, ...), custom_call_target="tpu_custom_call" | custom-call | tf_op jit(solution)/shard_map/pallas_call | solution.py:609
  74.4 1.9 %copy.11 = bf16[2,64,2048]{2,1,0:T(8,128)(2,1)} copy(bf16[2,64,2048]{2,1,0:T(8,128)(2,1)} %shard_map.91) | data formatting | bytes 1048576
